TPU v7x, 256 devices: a whole 4x4x8 slice. The times are simulated.
256 devices in a mesh: wide: 128 (over x, z, y_lo, core), narrow: 2 (over y_hi).
Axes of the slice: x: 4, y: 4 (y_hi: 2, y_lo: 2; y = y_hi * 2 + y_lo), z: 8, core: 2. Of those that a mesh axis runs over, the one named last changes fastest.
Arguments:
- frames: bfloat16 [131072, 768], P(('wide', 'narrow')), may hold values from -6 to 6
- down_kernel: bfloat16 [15, 768], replicated, may hold values from -1.5 to 1.5
- proj_weight: bfloat16 [768, 1024], P('wide'), may hold values from -0.21875 to 0.21875
- glu_weight: bfloat16 [1024, 2, 1024], P('wide', None, 'narrow'), may hold values from -0.1875 to 0.1875
- conv_kernel: bfloat16 [15, 1024], P(None, 'narrow'), may hold values from -1.5 to 1.5
- conv_out_weight: bfloat16 [1024, 1024], P('narrow', 'wide'), may hold values from -0.5 to 0.5
- ffn_in: bfloat16 [1024, 4096], P('wide', 'narrow'), may hold values from -0.1875 to 0.1875
- ffn_out: bfloat16 [4096, 1024], P('narrow', 'wide'), may hold values from -0.25 to 0.25
Outputs:
- section_out: bfloat16 [65536, 1024], P(('wide', 'narrow'))
All inputs are finite; a program needn't handle non-finite values.
Results may differ from a plain program's by a relative error of at most 0.017.
Values may be sent and summed in bfloat16 or wider, within the bound.
No kernel may reach another device: no remote copies, remote signals or barrier semaphores. Data moves between devices by JAX's collectives and lax.ppermute only.
A program may use at most 64 MiB of HBM per device.

v0:
```python
import jax
import jax.numpy as jnp
from jax import lax
from jax.sharding import PartitionSpec as P


def padded_2(x, sides, width):
    for axis, dim in sides:
        peers, length = (lax.axis_size(axis), x.shape[dim])
        up = [(i, (i + 1) % peers) for i in range(peers - 1)]
        down = [(j, i) for i, j in up]
        last = lax.slice_in_dim(x, length - width, length, axis=dim)
        leading = lax.slice_in_dim(x, 0, width, axis=dim)
        before = lax.ppermute(last, axis, up)
        after = lax.ppermute(leading, axis, down)
        x = jnp.concatenate([before, x, after], axis=dim)
    return x


def layer_norm(values):
    centre = jnp.mean(values, axis=-1, keepdims=True)
    centred = values - centre
    spread = jnp.mean(centred * centred, axis=-1, keepdims=True)
    return centred * lax.rsqrt(spread + 1e-05)


def body(
    frames, down_kernel, proj_weight, glu_weight, conv_kernel, conv_out_weight, ffn_in, ffn_out
):
    taps = down_kernel.shape[0]
    reach = taps // 2
    frame_rows = frames.shape[0]
    channels = frames.shape[1]
    padded = padded_2(frames, ((("wide", "narrow"), 0),), reach)
    padded_wide = padded.astype(jnp.float32)
    down_taps = down_kernel.astype(jnp.float32)
    reduced = jnp.zeros((frame_rows // 2, channels), jnp.float32)
    for offset in range(taps):
        window = lax.slice(padded_wide, (offset, 0), (offset + frame_rows - 1, channels), (2, 1))
        reduced = reduced + down_taps[offset] * window
    reduced = reduced.astype(jnp.bfloat16)
    source = lax.all_gather(reduced, "narrow", axis=0, tiled=True)
    empty = jnp.zeros((source.shape[0], proj_weight.shape[1]), jnp.float32)
    shard_piece = lax.all_gather(proj_weight, "wide", axis=0, tiled=True)
    columns = lax.slice_in_dim(source, 0, shard_piece.shape[0], axis=1)
    summed = empty + jnp.dot(columns, shard_piece, preferred_element_type=jnp.float32)
    projected = summed.astype(jnp.bfloat16)
    block_rows = projected.shape[0]
    normed = layer_norm(projected.astype(jnp.float32)).astype(jnp.bfloat16)
    glu_empty = jnp.zeros((block_rows, 2, glu_weight.shape[2]), jnp.float32)
    shard_piece = lax.all_gather(glu_weight, "wide", axis=0, tiled=True)
    columns = lax.slice_in_dim(normed, 0, shard_piece.shape[0], axis=1)
    glu_pre = glu_empty + jnp.einsum(
        "rc,cgh->rgh", columns, shard_piece, preferred_element_type=jnp.float32
    )
    gated = (glu_pre[:, 0, :] * jax.nn.sigmoid(glu_pre[:, 1, :])).astype(jnp.bfloat16)
    gated_pad = padded_2(gated, (("wide", 0),), reach).astype(jnp.float32)
    conv_taps = conv_kernel.astype(jnp.float32)
    depth = jnp.zeros(gated.shape, jnp.float32)
    for offset in range(taps):
        depth = depth + conv_taps[offset] * gated_pad[offset : offset + block_rows]
    activated = jax.nn.silu(depth).astype(jnp.bfloat16)
    conv_part = jnp.dot(
        activated,
        lax.all_gather(conv_out_weight, "wide", axis=1, tiled=True),
        preferred_element_type=jnp.float32,
    )
    half_rows = block_rows // 2
    own_start = lax.axis_index("narrow") * half_rows
    mixed = projected.astype(jnp.float32) + lax.psum(
        conv_part.astype(jnp.bfloat16), "narrow"
    ).astype(jnp.float32)
    own_mixed = lax.dynamic_slice_in_dim(mixed, own_start, half_rows, 0)
    second_norm = layer_norm(mixed).astype(jnp.bfloat16)
    ffn_empty = jnp.zeros((block_rows, ffn_in.shape[1]), jnp.float32)
    shard_piece = lax.all_gather(ffn_in, "wide", axis=0, tiled=True)
    columns = lax.slice_in_dim(second_norm, 0, shard_piece.shape[0], axis=1)
    hidden_pre = ffn_empty + jnp.dot(columns, shard_piece, preferred_element_type=jnp.float32)
    hidden = jax.nn.silu(hidden_pre).astype(jnp.bfloat16)
    ffn_part = jnp.dot(
        hidden,
        lax.all_gather(ffn_out, "wide", axis=1, tiled=True),
        preferred_element_type=jnp.float32,
    )
    ffn_share = lax.psum_scatter(
        ffn_part.astype(jnp.bfloat16), "narrow", scatter_dimension=0, tiled=True
    ).astype(jnp.float32)
    return (own_mixed + 0.5 * ffn_share).astype(jnp.bfloat16)


def solution(mesh):
    return jax.shard_map(
        body,
        mesh=mesh,
        in_specs=(
            P(("wide", "narrow"), None),
            P(),
            P("wide", None),
            P("wide", None, "narrow"),
            P(None, "narrow"),
            P("narrow", "wide"),
            P("wide", "narrow"),
            P("narrow", "wide"),
        ),
        out_specs=P(("wide", "narrow"), None),
        check_vma=False,
    )
```

profile of v0, /device:TPU:1, one launch (start us, length us, event | category | flops | bytes accessed | tf_op | source)
XLA Modules:
  0.0 1187.8 jit_solution(15642934463695296659)
XLA Ops:
  6.5 0.7 all-gather.15.cloned.1.call-update
  7.3 1.3 copy.11
  8.7 0.7 fusion.38
  9.4 5.6 collective-permute-start
  15.1 2.5 collective-permute-start.1
  17.6 0.7 convert_element_type.52
  18.4 1.0 fusion.39
  19.6 1.5 collective-permute-done.1
  21.0 1.3 maximum_convert_fusion
  22.3 0.7 slice.201
  23.0 0.7 slice.203
  23.7 2.8 slice.205
  26.5 2.8 slice.207
  29.3 2.8 slice.209
  32.2 2.8 slice.211
  35.0 2.8 slice.213
  37.8 2.8 slice.215
  40.5 2.7 slice.217
  43.3 2.8 slice.219
  46.1 2.8 slice.221
  48.9 2.8 slice.223
  51.7 2.8 slice.225
  54.5 2.8 slice.227
  57.3 2.8 slice.229
  60.1 4.8 add_convert_fusion.1
  64.9 10.7 all_gather.18
  75.6 149.7 %all-gather.15.cloned.1.call-done = bf16[128,6,1024]{2,1,0:T(8,128)(2,1)} async-done(((bf16[1,6,1024]{2,1,0:T(8,128)(2,1)}), bf16[128,6,1024]{2,1,0:T(8,128)(2,1)}) %all-gather.15.cloned.1.call-update) | async-done | bytes 1572880 | tf_op jit(solution)/shard_map/all_gather | solution.py:44
  225.3 2.6 reshape.35
  227.9 1.1 convert_reduce_fusion
  229.0 0.4 fusion.2
  229.4 210.3 %all-gather.7.cloned.1.call-done = bf16[1024,2,512]{2,0,1:T(8,128)(2,1)} async-done(((bf16[8,2,512]{2,0,1:T(8,128)(2,1)}), bf16[1024,2,512]{2,0,1:T(8,128)(2,1)}) %all-gather.7.cloned.1.call-update) | async-done | bytes 2097168 | tf_op jit(solution)/shard_map/all_gather | solution.py:51
  439.8 2.9 fusion.8
  442.7 0.3 fusion.34
  443.0 2.5 collective-permute-start.2
  445.4 1.9 collective-permute-start.3
  447.7 2.7 collective-permute-done.3
  450.6 200.3 %all-gather.9.cloned.1.call-done = bf16[512,1024]{0,1:T(8,128)(2,1)} async-done(((bf16[512,8]{0,1:T(8,128)(2,1)}), bf16[512,1024]{0,1:T(8,128)(2,1)}) %all-gather.9.cloned.1.call-update) | async-done | bytes 1048592 | tf_op jit(solution)/shard_map/all_gather | solution.py:65
  650.8 4.7 convolution_convert_fusion.1
  655.6 0.5 all-gather.11.cloned.1.call-update
  656.2 0.5 all-gather.13.cloned.1.call-update
  657.0 52.1 %all-reduce.2.cloned.1.call-done = bf16[512,1024]{1,0:T(8,128)(2,1)} async-done(((bf16[512,1024]{1,0:T(8,128)(2,1)}), bf16[512,1024]{1,0:T(8,128)(2,1)}) %all-reduce.2.cloned.1.call-update) | async-done | bytes 1048592 | tf_op jit(solution)/shard_map/psum | solution.py:70
  709.1 1.7 convert_add_fusion
  710.8 0.5 multiply_reduce_fusion
  711.3 214.3 %all-gather.11.cloned.1.call-done = bf16[1024,2048]{1,0:T(8,128)(2,1)} async-done(((bf16[8,2048]{1,0:T(8,128)(2,1)}), bf16[1024,2048]{1,0:T(8,128)(2,1)}) %all-gather.11.cloned.1.call-update) | async-done | bytes 4194320 | tf_op jit(solution)/shard_map/all_gather | solution.py:76
  925.6 216.9 %all-gather.13.cloned.1.call-done = bf16[2048,1024]{0,1:T(8,128)(2,1)} async-done(((bf16[2048,8]{0,1:T(8,128)(2,1)}), bf16[2048,1024]{0,1:T(8,128)(2,1)}) %all-gather.13.cloned.1.call-update) | async-done | bytes 4194320 | tf_op jit(solution)/shard_map/all_gather | solution.py:82
  1142.5 9.5 fusion.5
  1152.1 26.9 %reduce-scatter.2.cloned.1.call-done = bf16[256,1024]{1,0:T(8,128)(2,1)} async-done(((bf16[512,1024]{1,0:T(8,128)(2,1)}), bf16[256,1024]{1,0:T(8,128)(2,1)}) %reduce-scatter.2.cloned.1.call-update) | async-done | bytes 524304 | tf_op jit(solution)/shard_map/reduce_scatter | solution.py:85
  1179.0 2.0 add_convert_fusion
  (23 shorter events, 1.1 us)
Async XLA Ops:
  6.5 218.8 %all-gather.15.cloned.1.call-start = ((), (), s32[]{:S(2)}) async-start(), calls=%async_computation.7 | async-start | bytes 2113536 | tf_op jit(solution)/shard_map/all_gather | solution.py:44
  7.3 432.5 %all-gather.7.cloned.1.call-start = ((), (), s32[]{:S(2)}) async-start(), calls=%async_computation.1 | async-start | bytes 2113536 | tf_op jit(solution)/shard_map/all_gather | solution.py:51
  8.7 642.2 %all-gather.9.cloned.1.call-start = ((), (), s32[]{:S(2)}) async-start(), calls=%async_computation.2 | async-start | bytes 1056768 | tf_op jit(solution)/shard_map/all_gather | solution.py:65
  9.4 10.1 collective-permute-start
  15.1 5.9 collective-permute-start.1
  17.6 691.5 %all-reduce.2.cloned.1.call-start = ((), (), s32[]{:S(2)}) async-start(), calls=%async_computation.3 | async-start | bytes 2097152 | tf_op jit(solution)/shard_map/psum | solution.py:70
  443.0 4.7 collective-permute-start.2
  445.4 5.0 collective-permute-start.3
  655.6 270.0 %all-gather.11.cloned.1.call-start = ((), (), s32[]{:S(2)}) async-start(), calls=%async_computation.4 | async-start | bytes 4227072 | tf_op jit(solution)/shard_map/all_gather | solution.py:76
  656.2 486.3 %all-gather.13.cloned.1.call-start = ((), (), s32[]{:S(2)}) async-start(), calls=%async_computation.5 | async-start | bytes 4227072 | tf_op jit(solution)/shard_map/all_gather | solution.py:82
  656.8 522.2 %reduce-scatter.2.cloned.1.call-start = ((), (), s32[]{:S(2)}) async-start(), calls=%async_computation.6 | async-start | bytes 1572864 | tf_op jit(solution)/shard_map/reduce_scatter | solution.py:85
  709.1 1.7 copy-start
Sparse Core Ops, SparseCore 0:
  9.2 216.0 all-gather.14
  227.2 212.4 all-gather.6
  441.6 209.1 all-gather.8
  655.7 53.3 all-reduce.1
  711.0 214.6 all-gather.10
  927.5 214.9 all-gather.12
  1152.2 26.7 reduce-scatter.1
where the time goes:
time: 1190 us
  waiting for transfers between devices  1080 us (91%)
  local copies, waits for them, and re-layouts  43.6 us (4%)
  matrix products  18.2 us (2%)
  between operations  13.6 us (1%)
  starting transfers between devices  12.9 us (1%)
  other arithmetic  12.2 us (1%)
    all_gather x1, waiting for transfers between devices, body(): lax.all_gather(ffn_out, 'wide', axis=1, tiled=True)  217 us
    all_gather x1, waiting for transfers between devices, body(): shard_piece = lax.all_gather(ffn_in, 'wide', axis=0, tiled=True)  214 us
    all_gather x1, waiting for transfers between devices, body(): shard_piece = lax.all_gather(glu_weight, 'wide', axis=0, tiled=True)  210 us
    all_gather x1, waiting for transfers between devices, body(): lax.all_gather(conv_out_weight, 'wide', axis=1, tiled=True)  200 us
    all_gather x1, waiting for transfers between devices, body(): shard_piece = lax.all_gather(proj_weight, 'wide', axis=0, tiled=True)  150 us
    psum x1, waiting for transfers between devices, body(): lax.psum(conv_part.astype(jnp.bfloat16), 'narrow').astype(jnp.float32)  52.1 us
    slice x15, local copies, waits for them, and re-layouts, body(): lax.slice(padded_wide, (offset, 0), (offset + frame_rows - 1, channels),...  37.8 us
    reduce_scatter x1, waiting for transfers between devices, body(): lax.psum_scatter(ffn_part.astype(jnp.bfloat16), 'narrow', scatter_dimensi...  26.9 us
  transfers between devices with their start and end apart: 11, of which 9 were waited for; matrix products, arithmetic and copies ran while one was open for 5% of the time, Pallas kernels for 0%

commit v1 on v0

--- a/solution.py
+++ b/solution.py
@@ -73,7 +73,10 @@
     own_mixed = lax.dynamic_slice_in_dim(mixed, own_start, half_rows, 0)
     second_norm = layer_norm(mixed).astype(jnp.bfloat16)
     ffn_empty = jnp.zeros((block_rows, ffn_in.shape[1]), jnp.float32)
-    shard_piece = lax.all_gather(ffn_in, "wide", axis=0, tiled=True)
+    size = lax.axis_size("wide")
+    shards = jnp.stack([ffn_in for _ in range(size)])
+    shards = lax.all_to_all(shards, "wide", split_axis=0, concat_axis=0)
+    shard_piece = jnp.concatenate(shards, axis=0)
     columns = lax.slice_in_dim(second_norm, 0, shard_piece.shape[0], axis=1)
     hidden_pre = ffn_empty + jnp.dot(columns, shard_piece, preferred_element_type=jnp.float32)
     hidden = jax.nn.silu(hidden_pre).astype(jnp.bfloat16)

time: 1190 us -> 1000 us (0.84)
  waiting for transfers between devices: 1080 us -> 877 us
    all_gather x1 -> x0, waiting for transfers between devices: 214 us -> none  [body(): shard_piece = lax.all_gather(ffn_in, 'wide', axis=0, tiled=True)]
    all_gather x1, waiting for transfers between devices: 217 us -> 193 us  [body(): lax.all_gather(ffn_out, 'wide', axis=1, tiled=True)]
    all_to_all x0 -> x1, waiting for transfers between devices: none -> 22.3 us  [body(): shards = lax.all_to_all(shards, 'wide', split_axis=0, concat_axis=0)]
    psum x1, waiting for transfers between devices: 52.1 us -> 68.7 us  [body(): lax.psum(conv_part.astype(jnp.bfloat16), 'narrow').astype(jnp.float32)]
  transfers between devices with their start and end apart: 11 -> 11, of which waited for: 9 -> 9; matrix products, arithmetic and copies ran while one was open for 5% -> 6% of each run, Pallas kernels for 0% -> 0%
where the time goes in v1:
time: 1000 us
  waiting for transfers between devices  877 us (88%)
  local copies, waits for them, and re-layouts  46.1 us (5%)
  starting transfers between devices  23.6 us (2%)
  matrix products  18.3 us (2%)
  between operations  13.6 us (1%)
  other arithmetic  12.2 us (1%)
  blocking collectives  10.7 us (1%)
    all_gather x1, waiting for transfers between devices, body(): shard_piece = lax.all_gather(glu_weight, 'wide', axis=0, tiled=True)  210 us
    all_gather x1, waiting for transfers between devices, body(): lax.all_gather(conv_out_weight, 'wide', axis=1, tiled=True)  200 us
    all_gather x1, waiting for transfers between devices, body(): lax.all_gather(ffn_out, 'wide', axis=1, tiled=True)  193 us
    all_gather x1, waiting for transfers between devices, body(): shard_piece = lax.all_gather(proj_weight, 'wide', axis=0, tiled=True)  150 us
    psum x1, waiting for transfers between devices, body(): lax.psum(conv_part.astype(jnp.bfloat16), 'narrow').astype(jnp.float32)  68.7 us
    slice x15, local copies, waits for them, and re-layouts, body(): lax.slice(padded_wide, (offset, 0), (offset + frame_rows - 1, channels),...  37.8 us
    reduce_scatter x1, waiting for transfers between devices, body(): lax.psum_scatter(ffn_part.astype(jnp.bfloat16), 'narrow', scatter_dimensi...  27.4 us
    all_to_all x1, waiting for transfers between devices, body(): shards = lax.all_to_all(shards, 'wide', split_axis=0, concat_axis=0)  22.3 us
  transfers between devices with their start and end apart: 11, of which 9 were waited for; matrix products, arithmetic and copies ran while one was open for 6% of the time, Pallas kernels for 0%

profile of v1, /device:TPU:1, one launch (start us, length us, event | category | flops | bytes accessed | tf_op | source)
XLA Modules:
  0.0 1002.0 jit_solution(5685846175813376551)
XLA Ops:
  6.5 0.7 all-gather.12.cloned.1.call-update
  7.3 1.3 copy.11
  8.7 0.7 fusion.45
  9.4 5.6 collective-permute-start
  15.1 2.5 collective-permute-start.1
  17.6 0.7 convert_element_type.52
  18.4 1.0 fusion.46
  19.6 1.5 collective-permute-done.1
  21.0 1.3 maximum_convert_fusion
  22.3 0.7 slice.201
  23.0 0.7 slice.203
  23.7 2.8 slice.205
  26.5 2.8 slice.207
  29.3 2.8 slice.209
  32.2 2.8 slice.211
  35.0 2.8 slice.213
  37.8 2.8 slice.215
  40.5 2.7 slice.217
  43.3 2.8 slice.219
  46.1 2.8 slice.221
  48.9 2.8 slice.223
  51.7 2.8 slice.225
  54.5 2.8 slice.227
  57.3 2.8 slice.229
  60.1 4.8 add_convert_fusion.1
  64.9 10.7 %all_gather.15 = bf16[512,768]{1,0:T(8,128)(2,1)S(1)} all-gather(bf16[256,768]{1,0:T(8,128)(2,1)S(1)} %add_convert_fusion.1), channel_id=1, replica_groups=mesh['wide'=128,'narrow'=2] {'narrow'}, dimensions={0}, use_global_device_ids=true | all-gather | bytes 1179648 | tf_op jit(solution)/shard_map/all_gather | solution.py:42
  75.6 149.7 %all-gather.12.cloned.1.call-done = bf16[128,6,1024]{2,1,0:T(8,128)(2,1)} async-done(((bf16[1,6,1024]{2,1,0:T(8,128)(2,1)}), bf16[128,6,1024]{2,1,0:T(8,128)(2,1)}) %all-gather.12.cloned.1.call-update) | async-done | bytes 1572880 | tf_op jit(solution)/shard_map/all_gather | solution.py:44
  225.3 2.6 reshape.41
  227.9 1.1 convert_reduce_fusion
  229.0 0.4 fusion.4
  229.4 210.3 %all-gather.6.cloned.1.call-done = bf16[1024,2,512]{2,0,1:T(8,128)(2,1)} async-done(((bf16[8,2,512]{2,0,1:T(8,128)(2,1)}), bf16[1024,2,512]{2,0,1:T(8,128)(2,1)}) %all-gather.6.cloned.1.call-update) | async-done | bytes 2097168 | tf_op jit(solution)/shard_map/all_gather | solution.py:51
  439.8 2.9 fusion.15
  443.0 2.5 collective-permute-start.2
  445.4 1.9 collective-permute-start.3
  447.7 2.7 collective-permute-done.3
  450.6 200.3 %all-gather.8.cloned.1.call-done = bf16[512,1024]{0,1:T(8,128)(2,1)} async-done(((bf16[512,8]{0,1:T(8,128)(2,1)}), bf16[512,1024]{0,1:T(8,128)(2,1)}) %all-gather.8.cloned.1.call-update) | async-done | bytes 1048592 | tf_op jit(solution)/shard_map/all_gather | solution.py:65
  650.8 4.8 convolution_convert_fusion.1
  655.6 2.5 stack.2
  658.1 10.7 %all-to-all-start = ((bf16[128,8,2048]{2,1,0:T(8,128)(2,1)}), bf16[128,8,2048]{2,1,0:T(8,128)(2,1)}, u32[]{:S(2)}, u32[]{:S(2)}) async-start(bf16[128,8,2048]{2,1,0:T(8,128)(2,1)} %stack.2), calls=%async_computation | async-start | bytes 8388608 | tf_op jit(solution)/shard_map/all_to_all | solution.py:78
  668.8 0.5 all-gather.10.cloned.1.call-update
  669.6 68.7 %all-reduce.2.cloned.1.call-done = bf16[512,1024]{1,0:T(8,128)(2,1)} async-done(((bf16[512,1024]{1,0:T(8,128)(2,1)}), bf16[512,1024]{1,0:T(8,128)(2,1)}) %all-reduce.2.cloned.1.call-update) | async-done | bytes 1048592 | tf_op jit(solution)/shard_map/psum | solution.py:70
  738.3 1.7 convert_add_fusion
  740.0 0.5 multiply_reduce_fusion
  740.5 22.3 %all-to-all-done = bf16[128,8,2048]{2,1,0:T(8,128)(2,1)} async-done(((bf16[128,8,2048]{2,1,0:T(8,128)(2,1)}), bf16[128,8,2048]{2,1,0:T(8,128)(2,1)}, u32[]{:S(2)}, u32[]{:S(2)}) %all-to-all-start) | async-done | bytes 4194336 | tf_op jit(solution)/shard_map/all_to_all | solution.py:78
  762.8 193.2 %all-gather.10.cloned.1.call-done = bf16[2048,1024]{0,1:T(8,128)(2,1)} async-done(((bf16[2048,8]{0,1:T(8,128)(2,1)}), bf16[2048,1024]{0,1:T(8,128)(2,1)}) %all-gather.10.cloned.1.call-update) | async-done | bytes 4194320 | tf_op jit(solution)/shard_map/all_gather | solution.py:85
  956.0 9.6 fusion.11
  965.7 27.4 %reduce-scatter.2.cloned.1.call-done = bf16[256,1024]{1,0:T(8,128)(2,1)} async-done(((bf16[512,1024]{1,0:T(8,128)(2,1)}), bf16[256,1024]{1,0:T(8,128)(2,1)}) %reduce-scatter.2.cloned.1.call-update) | async-done | bytes 524304 | tf_op jit(solution)/shard_map/reduce_scatter | solution.py:88
  993.1 2.0 add_convert_fusion
  (25 shorter events, 1.4 us)
Async XLA Ops:
  6.5 218.8 %all-gather.12.cloned.1.call-start = ((), (), s32[]{:S(2)}) async-start(), calls=%async_computation.7 | async-start | bytes 2113536 | tf_op jit(solution)/shard_map/all_gather | solution.py:44
  7.3 432.5 %all-gather.6.cloned.1.call-start = ((), (), s32[]{:S(2)}) async-start(), calls=%async_computation.2 | async-start | bytes 2113536 | tf_op jit(solution)/shard_map/all_gather | solution.py:51
  8.7 642.2 %all-gather.8.cloned.1.call-start = ((), (), s32[]{:S(2)}) async-start(), calls=%async_computation.3 | async-start | bytes 1056768 | tf_op jit(solution)/shard_map/all_gather | solution.py:65
  9.4 10.1 %collective-permute-start = (bf16[7,768]{1,0:T(8,128)(2,1)S(1)}, bf16[7,768]{1,0:T(8,128)(2,1)S(1)}, u32[]{:S(2)}, u32[]{:S(2)}) collective-permute-start(bf16[7,768]{1,0:T(8,128)(2,1)S(1)} %get-tuple-element.22), channel_id=1, source_target_pairs={{0,1},{1,2},{2,3},{3,4},{4,5},{5,6},{6,7},{7,8},{8,9},{9,10},{10,1... | collective-permute-start | bytes 32264 | tf_op jit(solution)/shard_map/ppermute | solution.py:14
  15.1 5.9 collective-permute-start.1
  17.6 720.7 %all-reduce.2.cloned.1.call-start = ((), (), s32[]{:S(2)}) async-start(), calls=%async_computation.4 | async-start | bytes 2097152 | tf_op jit(solution)/shard_map/psum | solution.py:70
  443.0 4.7 collective-permute-start.2
  445.4 5.0 collective-permute-start.3
  650.8 4.8 copy-start.1
  658.1 104.7 %all-to-all-start = ((bf16[128,8,2048]{2,1,0:T(8,128)(2,1)}), bf16[128,8,2048]{2,1,0:T(8,128)(2,1)}, u32[]{:S(2)}, u32[]{:S(2)}) async-start(bf16[128,8,2048]{2,1,0:T(8,128)(2,1)} %stack.2), calls=%async_computation | async-start | bytes 8388608 | tf_op jit(solution)/shard_map/all_to_all | solution.py:78
  668.8 287.2 %all-gather.10.cloned.1.call-start = ((), (), s32[]{:S(2)}) async-start(), calls=%async_computation.5 | async-start | bytes 4227072 | tf_op jit(solution)/shard_map/all_gather | solution.py:85
  669.4 323.7 %reduce-scatter.2.cloned.1.call-start = ((), (), s32[]{:S(2)}) async-start(), calls=%async_computation.6 | async-start | bytes 1572864 | tf_op jit(solution)/shard_map/reduce_scatter | solution.py:88
  738.3 1.7 copy-start
Sparse Core Ops, SparseCore 0:
  9.2 216.0 all-gather.11
  227.2 212.4 all-gather.5
  441.6 209.1 all-gather.7
  655.7 82.5 all-reduce.1
  740.2 215.7 all-gather.9
  965.8 27.2 reduce-scatter.1
